TPU v7x, 512 devices: a whole 4x4x16 slice. The times are simulated.
512 devices in a mesh: dp: 16 (over z), expert: 32 (over x, y, core).
Axes of the slice: x: 4, y: 4, z: 16, core: 2. Of those that a mesh axis runs over, the one named last changes fastest.
Arguments:
- tokens: bfloat16 [65536, 1024], P(('dp', 'expert')), may hold values from -6 to 6
- route_ids: int32 [65536, 4], P(('dp', 'expert')), may hold values from 0 to 31, all different within a row; in each aligned block of 128 rows (0 to 127, 128 to 255, ...) at most 24 rows name the same one
- route_weights: float32 [65536, 4], P(('dp', 'expert')), may hold values from 0.2 to 1
- up_weight: bfloat16 [32, 1024, 704], P('expert', 'dp'), may hold values from -0.1875 to 0.1875
- down_weight: bfloat16 [32, 1024, 704], P('expert', 'dp'), may hold values from -0.21875 to 0.21875
- head_weight: bfloat16 [1024, 1024], P('dp'), may hold values from -0.75 to 0.75
- out_weight: float32 [1024], P('dp'), may hold values from -0.375 to 0.375
- pool_ids: int32 [512, 128], P(('dp', 'expert')), may hold values from 0 to 15, never falling along the last dimension, each value on 1 to 64 neighbouring positions
- list_ids: int32 [512, 16], P(('dp', 'expert')), may hold values from 0 to 7, as said below
- clicks: int32 [512, 16], P(('dp', 'expert')), may hold values 0 or 1
- ranks: int32 [512, 16], P(('dp', 'expert')), may hold values from 0 to 31
- alpha_table: float32 [32], replicated, may hold values from 0.3 to 1
- beta_table: float32 [32], replicated, may hold values from 0 to 0.3
Outputs:
- grad_up: bfloat16 [32, 1024, 704], P('expert', 'dp')
- grad_down: bfloat16 [32, 1024, 704], P('expert', 'dp')
- grad_head: float32 [1024, 1024], P('dp')
- grad_out: float32 [1024], P('dp')
- list_loss: float32 [32], P('expert')
Inputs may be any that keep to these rules, and one draw needn't show every extreme that they name: `route_ids`: each token names 4 different experts; among the 128 tokens of one device no expert is named more than 24 times, a bound that some block reaches. `pool_ids`: in each row the candidate number never falls, every candidate has 1 to 64 tokens and one has exactly 64. `list_ids`: every list number appears in every row.
All inputs are finite; a program needn't handle non-finite values. No bound on the sum of `clicks` on one device may be relied on, other than what follows from the above.
Results may differ from a plain program's by a relative error of at most 0.028.
Values may be sent and summed in bfloat16 or wider, within the bound.
A program may use at most 64 MiB of HBM per device.

v0:
```python
import jax
import jax.numpy as jnp
from jax import lax
from jax.sharding import PartitionSpec as P

LISTS = 8
RANKS = 32


def silu_slope(pre_act):
    sigmoid = jax.nn.sigmoid(pre_act)
    return sigmoid * (1.0 + pre_act * (1.0 - sigmoid))


def local(
    tokens,
    route_ids,
    route_weights,
    up_weight,
    down_weight,
    head_weight,
    out_weight,
    pool_ids,
    list_ids,
    clicks,
    ranks,
    alpha_table,
    beta_table,
):
    tok_count = tokens.shape[0]
    model_width = tokens.shape[1]
    top_count = route_ids.shape[1]
    owners = lax.axis_size("expert")
    capacity = 3 * tok_count * top_count // (2 * owners)
    slot_total = owners * capacity
    flat_ids = route_ids.reshape(-1)
    expert_hot = (flat_ids[:, None] == jnp.arange(owners, dtype=jnp.int32)[None, :]).astype(
        jnp.int32
    )
    running = jnp.cumsum(expert_hot, axis=0) - 1
    slot_index = jnp.sum(running * expert_hot, axis=1)
    target = flat_ids * capacity + slot_index
    token_index = jnp.arange(tok_count * top_count, dtype=jnp.int32) // top_count
    outgoing = (
        jnp.zeros((slot_total, model_width), jnp.bfloat16).at[target].set(tokens[token_index])
    )
    received = lax.all_to_all(
        outgoing.reshape(owners, capacity, model_width),
        "expert",
        split_axis=0,
        concat_axis=0,
        tiled=True,
    )
    inputs = received.reshape(slot_total, model_width)
    up_local = up_weight[0]
    down_local = down_weight[0]
    hidden_width = up_local.shape[1]
    columns = inputs
    pre_act = jnp.dot(
        columns,
        lax.all_gather(up_local, "dp", axis=0, tiled=True),
        preferred_element_type=jnp.float32,
    )
    activated = jax.nn.silu(pre_act).astype(jnp.bfloat16)
    expert_out = lax.dot_general(
        activated,
        lax.all_gather(down_local, "dp", axis=0, tiled=True),
        (((1,), (1,)), ((), ())),
        preferred_element_type=jnp.float32,
    ).astype(jnp.bfloat16)
    returned = lax.all_to_all(
        expert_out.reshape(owners, capacity, model_width),
        "expert",
        split_axis=0,
        concat_axis=0,
        tiled=True,
    ).reshape(slot_total, model_width)
    routed_rows = returned[target].reshape(tok_count, top_count, model_width)
    routed = jnp.sum(route_weights[:, :, None] * routed_rows.astype(jnp.float32), axis=1)
    mixed = tokens.astype(jnp.float32) + routed
    inv_rms = lax.rsqrt(jnp.mean(mixed * mixed, axis=1, keepdims=True) + 1e-06)
    normed = mixed * inv_rms
    cand_count = list_ids.shape[1]
    member = (pool_ids[0][:, None] == jnp.arange(cand_count, dtype=jnp.int32)[None, :]).astype(
        jnp.float32
    )
    token_counts = jnp.sum(member, axis=0)
    pooled_sum = lax.dot_general(
        member,
        normed,
        (((0,), (0,)), ((), ())),
        precision=lax.Precision.HIGHEST,
        preferred_element_type=jnp.float32,
    )
    pooled = (pooled_sum / token_counts[:, None]).astype(jnp.bfloat16)
    all_pooled = lax.all_gather(pooled, "dp", axis=0, tiled=True)
    head_act = jnp.tanh(
        lax.dot_general(
            all_pooled, head_weight, (((1,), (1,)), ((), ())), preferred_element_type=jnp.float32
        )
    )
    part_score = jnp.sum(head_act * out_weight[None, :], axis=1)
    rank_hot = (ranks[0][:, None] == jnp.arange(RANKS, dtype=jnp.int32)[None, :]).astype(
        jnp.float32
    )
    alpha_of = jnp.sum(rank_hot * alpha_table[None, :], axis=1)
    beta_of = jnp.sum(rank_hot * beta_table[None, :], axis=1)
    corrected = (clicks[0].astype(jnp.float32) - beta_of) / alpha_of
    list_hot = (list_ids[0][:, None] == jnp.arange(LISTS, dtype=jnp.int32)[None, :]).astype(
        jnp.float32
    )
    scores = lax.psum_scatter(part_score, "dp", scatter_dimension=0, tiled=True)
    exp_scores = jnp.exp(scores)
    exp_total, click_total, cross_total = lax.psum(
        (
            jnp.sum(exp_scores[:, None] * list_hot, axis=0),
            jnp.sum(corrected[:, None] * list_hot, axis=0),
            jnp.sum((corrected * scores)[:, None] * list_hot, axis=0),
        ),
        "dp",
    )
    list_loss = jnp.sum(click_total * jnp.log(exp_total) - cross_total).reshape(1)
    cand_grad = (
        jnp.sum(list_hot * (click_total / exp_total)[None, :], axis=1) * exp_scores - corrected
    )
    group_grad = lax.all_gather(cand_grad, "dp", axis=0, tiled=True)
    hid_grad = (group_grad[:, None] * out_weight[None, :] * (1.0 - head_act * head_act)).astype(
        jnp.bfloat16
    )
    head_term = lax.dot_general(
        hid_grad, all_pooled, (((0,), (0,)), ((), ())), preferred_element_type=jnp.float32
    )
    out_term = jnp.sum(group_grad[:, None] * head_act, axis=0)
    grad_head, grad_out = (
        lax.psum(head_term.astype(jnp.bfloat16), "expert").astype(jnp.float32),
        lax.psum(out_term.astype(jnp.bfloat16), "expert").astype(jnp.float32),
    )
    pooled_grad = lax.psum_scatter(
        jnp.dot(hid_grad, head_weight, preferred_element_type=jnp.float32).astype(jnp.bfloat16),
        "dp",
        scatter_dimension=0,
        tiled=True,
    ).astype(jnp.float32)
    normed_grad = jnp.dot(
        member,
        pooled_grad / token_counts[:, None],
        precision=lax.Precision.HIGHEST,
        preferred_element_type=jnp.float32,
    )
    mixed_grad = inv_rms * (
        normed_grad - normed * jnp.mean(normed_grad * normed, axis=1, keepdims=True)
    )
    cotangent = (
        (route_weights[:, :, None] * mixed_grad[:, None, :])
        .astype(jnp.bfloat16)
        .reshape(tok_count * top_count, model_width)
    )
    outgoing_grad = jnp.zeros((slot_total, model_width), jnp.bfloat16).at[target].set(cotangent)
    slot_grad = lax.all_to_all(
        outgoing_grad.reshape(owners, capacity, model_width),
        "expert",
        split_axis=0,
        concat_axis=0,
        tiled=True,
    ).reshape(slot_total, model_width)
    columns = slot_grad
    act_grad = jnp.dot(
        columns,
        lax.all_gather(down_local, "dp", axis=0, tiled=True),
        preferred_element_type=jnp.float32,
    )
    pre_grad = (act_grad * silu_slope(pre_act)).astype(jnp.bfloat16)
    up_term = lax.dot_general(
        inputs, pre_grad, (((0,), (0,)), ((), ())), preferred_element_type=jnp.float32
    )
    down_term = lax.dot_general(
        slot_grad, activated, (((0,), (0,)), ((), ())), preferred_element_type=jnp.float32
    )
    summed = lax.psum_scatter(
        jnp.concatenate([up_term, down_term], axis=1).astype(jnp.bfloat16),
        "dp",
        scatter_dimension=0,
        tiled=True,
    ).astype(jnp.float32)
    grad_up = summed[:, :hidden_width].astype(jnp.bfloat16)[None]
    grad_down = summed[:, hidden_width:].astype(jnp.bfloat16)[None]
    return (grad_up, grad_down, grad_head, grad_out, list_loss)


def solution(mesh):
    return jax.shard_map(
        local,
        mesh=mesh,
        in_specs=(
            P(("dp", "expert"), None),
            P(("dp", "expert"), None),
            P(("dp", "expert"), None),
            P("expert", "dp", None),
            P("expert", "dp", None),
            P("dp", None),
            P("dp"),
            P(("dp", "expert"), None),
            P(("dp", "expert"), None),
            P(("dp", "expert"), None),
            P(("dp", "expert"), None),
            P(),
            P(),
        ),
        out_specs=(
            P("expert", "dp", None),
            P("expert", "dp", None),
            P("dp", None),
            P("dp"),
            P("expert"),
        ),
        check_vma=False,
    )
```

profile of v0, /device:TPU:2, one launch (start us, length us, event | category | flops | bytes accessed | tf_op | source)
XLA Modules:
  0.0 616.2 jit_solution(5484869024064051022)
XLA Ops:
  7.2 0.7 all-gather.5.cloned.1.call-update
  8.0 0.7 all-gather.7.cloned.1.call-update
  8.7 0.7 broadcast_multiply_fusion
  9.4 0.8 copy.38
  10.1 0.1 eq.74
  10.2 0.1 eq.70
  10.4 0.1 copy.37
  10.5 0.1 mul.176
  10.6 1.2 reduce-window.6
  11.8 0.2 slice_reduce_fusion
  12.2 7.4 %scatter_custom_fusion = bf16[768,1024]{1,0:T(8,128)(2,1)S(1)} fusion(s32[512]{0:T(512)S(1)} %bitcast.67, bf16[128,1024]{1,0:T(8,128)(2,1)} %param.13, s32[1024]{0:T(1024)S(1)} %pad_clamp_fusion.1, bf16[]{:T(256)} %constant.40.clone.1), kind=kCustom, calls=%fused_computation.24 | custom fusion | bytes 1573376 | tf_op jit(solution)/shard_map/scatter | solution.py:45
  19.6 29.6 %all_to_all.15 = bf16[32,24,1024]{2,1,0:T(8,128)(2,1)S(1)} all-to-all(bf16[32,24,1024]{2,1,0:T(8,128)(2,1)S(1)} %bitcast.60), channel_id=1, replica_groups=mesh['dp'=16,'expert'=32] {'expert'}, dimensions={0} | all-to-all | bytes 3145728 | tf_op jit(solution)/shard_map/all_to_all | solution.py:47
  49.2 37.5 %all-gather.5.cloned.1.call-done = bf16[1,1024,704]{2,1,0:T(8,128)(2,1)} async-done(((bf16[1,64,704]{2,1,0:T(8,128)(2,1)}), bf16[1,1024,704]{2,1,0:T(8,128)(2,1)}) %all-gather.5.cloned.1.call-update) | async-done | bytes 1441808 | tf_op jit(solution)/shard_map/all_gather | solution.py:61
  86.7 4.1 fusion.2
  90.8 67.2 %all-gather.7.cloned.1.call-done = bf16[1,1024,704]{2,1,0:T(8,128)(2,1)} async-done(((bf16[1,64,704]{2,1,0:T(8,128)(2,1)}), bf16[1,1024,704]{2,1,0:T(8,128)(2,1)}) %all-gather.7.cloned.1.call-update) | async-done | bytes 1441808 | tf_op jit(solution)/shard_map/all_gather | solution.py:67
  158.0 4.7 convolution_convert_fusion
  162.7 7.6 %all-to-all-start.1 = ((bf16[32,24,1024]{2,1,0:T(8,128)(2,1)}), bf16[32,24,1024]{2,1,0:T(8,128)(2,1)S(1)}, u32[]{:S(2)}, u32[]{:S(2)}) async-start(bf16[32,24,1024]{2,1,0:T(8,128)(2,1)} %bitcast.8), calls=%async_computation.1 | async-start | bytes 3145728 | tf_op jit(solution)/shard_map/all_to_all | solution.py:71
  170.3 0.2 reduce-scatter.5.cloned.1.call-start
  170.5 0.7 copy.41
  171.3 0.6 fusion.29
  173.2 0.6 convert_reduce_fusion
  173.8 0.7 select_reduce_fusion.1
  174.5 15.9 %all-to-all-done.1 = bf16[32,24,1024]{2,1,0:T(8,128)(2,1)S(1)} async-done(((bf16[32,24,1024]{2,1,0:T(8,128)(2,1)}), bf16[32,24,1024]{2,1,0:T(8,128)(2,1)S(1)}, u32[]{:S(2)}, u32[]{:S(2)}) %all-to-all-start.1) | async-done | bytes 1572896 | tf_op jit(solution)/shard_map/all_to_all | solution.py:71
  190.4 2.8 gather_fusion
  193.2 1.8 reshape.174
  195.0 1.3 multiply_reduce_fusion
  196.4 0.2 multiply_reduce_fusion.2
  196.6 0.4 fusion.4
  197.0 31.4 %all_gather.15 = bf16[256,1024]{1,0:T(8,128)(2,1)S(1)} all-gather(bf16[16,1024]{1,0:T(8,128)(2,1)S(1)} %fusion.4), channel_id=1, replica_groups=mesh['dp'=16,'expert'=32] {'dp'}, dimensions={0}, use_global_device_ids=true | all-gather | bytes 557056 | tf_op jit(solution)/shard_map/all_gather | solution.py:96
  228.4 0.3 multiply_reduce_fusion.4
  228.7 27.0 %all-reduce.1 = f32[256]{0:T(256)S(1)} all-reduce(f32[256]{0:T(256)S(1)} %get-tuple-element.42), channel_id=4, replica_groups=mesh['dp'=16,'expert'=32] {'dp'}, use_global_device_ids=true, to_apply=%region_12.13.clone | all-reduce | flops 256 | bytes 2048
  255.8 0.1 select_reduce_fusion.4
  256.0 29.0 %all-reduce.3 = (f32[8]{0:T(128)S(1)}, f32[8]{0:T(128)S(1)}) all-reduce(f32[8]{0:T(128)S(1)} %get-tuple-element.28, f32[8]{0:T(128)S(1)} %get-tuple-element.27), channel_id=1, replica_groups=mesh['dp'=16,'expert'=32] {'dp'}, use_global_device_ids=true, to_apply=%region_9.10 | all-reduce | flops 16 | bytes 128 | tf_op jit(solution)/shard_map/psum | solution.py:114
  285.0 0.1 select_reduce_fusion.2
  285.1 0.1 subtract_dynamic-update-slice_fusion
  285.2 27.6 %all-reduce.2 = (f32[256]{0:T(256)S(1)}, f32[8]{0:T(128)}) all-reduce(f32[256]{0:T(256)S(1)} %subtract_dynamic-update-slice_fusion, f32[8]{0:T(128)S(1)} %get-tuple-element.25), channel_id=1, replica_groups=mesh['dp'=16,'expert'=32] {'dp'}, use_global_device_ids=true, to_apply=%add | all-reduce | flops 264 | bytes 2112
  312.8 1.2 convolution_convert_fusion.3
  314.0 0.1 mul.178
  314.1 64.8 %reduce-scatter.5.cloned.1.call-done = bf16[16,1024]{1,0:T(8,128)(2,1)} async-done(((bf16[256,1024]{1,0:T(8,128)(2,1)}), bf16[16,1024]{1,0:T(8,128)(2,1)}) %reduce-scatter.5.cloned.1.call-update) | async-done | bytes 32784 | tf_op jit(solution)/shard_map/reduce_scatter | solution.py:138
  378.9 1.3 multiply_reduce_fusion.1
  380.2 0.2 subtract_multiply_fusion
  380.4 1.9 mul.207
  382.3 2.0 mul.208
  384.3 3.9 scatter_custom_fusion.1
  388.2 7.5 %all-to-all-start.2 = ((bf16[32,24,1024]{2,1,0:T(8,128)(2,1)}), bf16[32,24,1024]{2,1,0:T(8,128)(2,1)S(1)}, u32[]{:S(2)}, u32[]{:S(2)}) async-start(bf16[32,24,1024]{2,1,0:T(8,128)(2,1)} %bitcast.59), calls=%async_computation.3 | async-start | bytes 3145728 | tf_op jit(solution)/shard_map/all_to_all | solution.py:159
  395.8 0.9 convolution_convert_fusion.4
  396.7 0.3 reduce-scatter.7.cloned.1.call-start
  397.0 18.9 %all-to-all-done.2 = bf16[32,24,1024]{2,1,0:T(8,128)(2,1)S(1)} async-done(((bf16[32,24,1024]{2,1,0:T(8,128)(2,1)}), bf16[32,24,1024]{2,1,0:T(8,128)(2,1)S(1)}, u32[]{:S(2)}, u32[]{:S(2)}) %all-to-all-start.2) | async-done | bytes 1572896 | tf_op jit(solution)/shard_map/all_to_all | solution.py:159
  415.9 4.2 convolution_convert_fusion.1
  420.0 6.6 %convolution_convert_fusion.2 = bf16[1024,704]{0,1:T(8,128)(2,1)} fusion(bf16[768,1024]{1,0:T(8,128)(2,1)S(1)} %bitcast.62, f32[768,704]{0,1:T(8,128)} %fusion.2, bf16[768,1024]{1,0:T(8,128)(2,1)S(1)} %bitcast.64, bf16[1,1024,704]{2,1,0:T(8,128)(2,1)} %all-gather.7.cloned.1.call-done), kind=kOutput, calls=%fused_computation.12 | convolution fusion | flops 2220179456 | bytes 8192000 | tf_op jit(solution)/shard_map/dot_general | solution.py:173
  426.6 2.1 pad_maximum_fusion
  428.7 2.9 copy.45
  431.6 0.1 multiply_reduce_fusion.3
  431.7 56.4 %psum.38 = bf16[64]{0:T(256)(128)(2,1)S(1)} all-reduce(bf16[64]{0:T(256)(128)(2,1)S(1)} %multiply_reduce_fusion.3), channel_id=1, replica_groups=mesh['dp'=16,'expert'=32] {'expert'}, use_global_device_ids=true, to_apply=%region_22.23 | all-reduce | flops 64 | bytes 256 | tf_op jit(solution)/shard_map/psum | solution.py:136
  488.1 0.5 convert_element_type.88
  488.6 0.6 subtract_reduce_fusion
  489.2 39.0 %all-reduce.6.cloned.1.call-done = bf16[64,1024]{1,0:T(8,128)(2,1)} async-done(((bf16[64,1024]{1,0:T(8,128)(2,1)}), bf16[64,1024]{1,0:T(8,128)(2,1)}) %all-reduce.6.cloned.1.call-update) | async-done | bytes 131088 | tf_op jit(solution)/shard_map/psum | solution.py:135
  528.2 1.6 convert_element_type.86
  529.8 76.8 %reduce-scatter.7.cloned.1.call-done = bf16[64,1408]{1,0:T(8,128)(2,1)} async-done(((bf16[1024,1408]{1,0:T(8,128)(2,1)}), bf16[64,1408]{1,0:T(8,128)(2,1)}) %reduce-scatter.7.cloned.1.call-update) | async-done | bytes 180240
  606.7 1.1 fusion.28
  607.8 0.2 copy.48
  607.9 0.8 copy.44
  608.7 0.2 copy.47
  608.9 0.8 copy.43
  (67 shorter events, 0.6 us)
Async XLA Ops:
  7.2 221.2 %copy-start = (bf16[64,1024]{1,0:T(8,128)(2,1)S(1)}, bf16[64,1024]{1,0:T(8,128)(2,1)}, u32[]{:S(2)}) copy-start(bf16[64,1024]{1,0:T(8,128)(2,1)} %param.18) | copy-start | bytes 393220
  7.2 79.5 %all-gather.5.cloned.1.call-start = ((), (), s32[]{:S(2)}) async-start(), calls=%async_computation.7 | async-start | bytes 1671168 | tf_op jit(solution)/shard_map/all_gather | solution.py:61
  7.9 150.1 %all-gather.7.cloned.1.call-start = ((), (), s32[]{:S(2)}) async-start(), calls=%async_computation.8 | async-start | bytes 1671168 | tf_op jit(solution)/shard_map/all_gather | solution.py:67
  49.2 41.6 %copy-start.2 = (bf16[32,24,1024]{2,1,0:T(8,128)(2,1)}, bf16[32,24,1024]{2,1,0:T(8,128)(2,1)S(1)}, u32[]{:S(2)}) copy-start(bf16[32,24,1024]{2,1,0:T(8,128)(2,1)S(1)} %all_to_all.15) | copy-start | bytes 4718596
  162.6 7.9 %copy-start.9 = (f32[128,4]{0,1:T(4,128)S(1)}, f32[128,4]{0,1:T(4,128)}, u32[]{:S(2)}) copy-start(f32[128,4]{0,1:T(4,128)} %param.15) | copy-start | bytes 6148
  162.6 8.6 %copy-start.16 = (u32[512]{0:T(512)S(1)}, u32[512]{0:T(512)}, u32[]{:S(2)}) copy-start(u32[512]{0:T(512)} %constant.64) | copy-start | bytes 6148
  162.6 10.5 %copy-start.12 = (s32[1,128]{1,0:T(1,128)S(1)}, s32[1,128]{1,0:T(1,128)}, u32[]{:S(2)}) copy-start(s32[1,128]{1,0:T(1,128)} %param.20) | copy-start | bytes 1540
  162.6 11.1 %copy-start.17 = (f32[32]{0:T(128)S(1)}, f32[32]{0:T(128)}, u32[]{:S(2)}) copy-start(f32[32]{0:T(128)} %param.25) | copy-start | bytes 388
  162.7 11.1 %copy-start.18 = (s32[1,16]{1,0:T(1,128)S(1)}, s32[1,16]{1,0:T(1,128)}, u32[]{:S(2)}) copy-start(s32[1,16]{1,0:T(1,128)} %param.23) | copy-start | bytes 196
  162.7 11.1 %copy-start.19 = (f32[32]{0:T(128)S(1)}, f32[32]{0:T(128)}, u32[]{:S(2)}) copy-start(f32[32]{0:T(128)} %param.24) | copy-start | bytes 388
  162.7 27.7 %all-to-all-start.1 = ((bf16[32,24,1024]{2,1,0:T(8,128)(2,1)}), bf16[32,24,1024]{2,1,0:T(8,128)(2,1)S(1)}, u32[]{:S(2)}, u32[]{:S(2)}) async-start(bf16[32,24,1024]{2,1,0:T(8,128)(2,1)} %bitcast.8), calls=%async_computation.1 | async-start | bytes 3145728 | tf_op jit(solution)/shard_map/all_to_all | solution.py:71
  170.3 208.6 %reduce-scatter.5.cloned.1.call-start = ((), (), s32[]{:S(2)}) async-start(), calls=%async_computation.5 | async-start | bytes 557056 | tf_op jit(solution)/shard_map/reduce_scatter | solution.py:138
  193.2 1.8 copy-start.6
  194.9 1.4 copy-start.1
  195.0 1.6 copy-start.14
  196.3 32.0 %copy-start.8 = (f32[64]{0:T(128)S(1)}, f32[64]{0:T(128)}, u32[]{:S(2)}) copy-start(f32[64]{0:T(128)} %param.19) | copy-start | bytes 772
  196.3 59.4 %copy-start.11 = (f32[16]{0:T(128)S(1)}, f32[16]{0:T(128)}, u32[]{:S(2)}) copy-start(f32[16]{0:T(128)} %get-tuple-element.30) | copy-start | bytes 196
  196.4 59.4 %copy-start.23 = (s32[1,16]{1,0:T(1,128)S(1)}, s32[1,16]{1,0:T(1,128)}, u32[]{:S(2)}) copy-start(s32[1,16]{1,0:T(1,128)} %param.22) | copy-start | bytes 196
  196.4 59.4 %copy-start.10 = (s32[1,16]{1,0:T(1,128)S(1)}, s32[1,16]{1,0:T(1,128)}, u32[]{:S(2)}) copy-start(s32[1,16]{1,0:T(1,128)} %param.21) | copy-start | bytes 196
  196.6 117.5 %copy-start.7 = (f32[128,4]{1,0:T(8,128)S(1)}, f32[128,4]{1,0:T(8,128)}, u32[]{:S(2)}) copy-start(f32[128,4]{1,0:T(8,128)} %copy.41) | copy-start | bytes 6148
  196.6 182.3 %copy-start.13 = (s32[1,128]{1,0:T(1,128)S(1)}, s32[1,128]{1,0:T(1,128)}, u32[]{:S(2)}) copy-start(s32[1,128]{1,0:T(1,128)} %param.20) | copy-start | bytes 1540
  196.6 182.3 %copy-start.15 = (f32[16]{0:T(128)S(1)}, f32[16]{0:T(128)}, u32[]{:S(2)}) copy-start(f32[16]{0:T(128)} %convert_reduce_fusion) | copy-start | bytes 196
  228.7 151.5 %copy-start.4 = (f32[256,64]{0,1:T(8,128)}, f32[256,64]{0,1:T(8,128)S(1)}, u32[]{:S(2)}) copy-start(f32[256,64]{0,1:T(8,128)S(1)} %get-tuple-element.43) | copy-start | bytes 196612
  285.0 95.4 %copy-start.20 = (f32[8]{0:T(128)}, f32[8]{0:T(128)S(1)}, u32[]{:S(2)}) copy-start(f32[8]{0:T(128)S(1)} %get-tuple-element.34) | copy-start | bytes 100
  388.2 7.6 %copy-start.5 = (f32[256,64]{0,1:T(8,128)S(1)}, f32[256,64]{0,1:T(8,128)}, u32[]{:S(2)}) copy-start(f32[256,64]{0,1:T(8,128)} %copy-done.4) | copy-start | bytes 196612
  388.2 27.7 %all-to-all-start.2 = ((bf16[32,24,1024]{2,1,0:T(8,128)(2,1)}), bf16[32,24,1024]{2,1,0:T(8,128)(2,1)S(1)}, u32[]{:S(2)}, u32[]{:S(2)}) async-start(bf16[32,24,1024]{2,1,0:T(8,128)(2,1)} %bitcast.59), calls=%async_computation.3 | async-start | bytes 3145728 | tf_op jit(solution)/shard_map/all_to_all | solution.py:159
  395.8 132.5 %all-reduce.6.cloned.1.call-start = ((), (), s32[]{:S(2)}) async-start(), calls=%async_computation.6 | async-start | bytes 262144 | tf_op jit(solution)/shard_map/psum | solution.py:135
  396.7 209.9 %reduce-scatter.7.cloned.1.call-start = ((), (), s32[]{:S(2)}) async-start(), calls=%async_computation.9 | async-start | bytes 3063808
  415.9 4.2 copy-start.3
  431.6 57.0 %copy-start.21 = (f32[8]{0:T(128)S(1)}, f32[8]{0:T(128)}, u32[]{:S(2)}) copy-start(f32[8]{0:T(128)} %copy-done.20) | copy-start | bytes 100
  431.6 57.0 %copy-start.22 = (f32[8]{0:T(128)S(1)}, f32[8]{0:T(128)}, u32[]{:S(2)}) copy-start(f32[8]{0:T(128)} %get-tuple-element.32) | copy-start | bytes 100
Sparse Core Ops, SparseCore 0:
  10.1 76.5 all-gather.4
  88.7 69.1 all-gather.6
  314.2 64.6 reduce-scatter.4
  400.4 127.7 all-reduce.5
  530.9 75.7 reduce-scatter.6
where the time goes:
time: 617 us; the launch traced here: 616 us
  waiting for transfers between devices  321 us (52%)
  blocking collectives  201 us (33%)
  local copies, waits for them, and re-layouts  24.7 us (4%)
  matrix products  23.6 us (4%)
  starting transfers between devices  15.7 us (3%)
  between operations  15.4 us (2%)
  other arithmetic  14.4 us (2%)
    unnamed x6, waiting for transfers between devices  78.3 us
    all_gather x1, waiting for transfers between devices, local(): lax.all_gather(down_local, 'dp', axis=0, tiled=True)  67.2 us
    reduce_scatter x1, waiting for transfers between devices, local(): lax.psum_scatter(jnp.dot(hid_grad, head_weight, preferred_element_type=jn...  64.8 us
    psum x1, blocking collectives, local(): lax.psum(out_term.astype(jnp.bfloat16), 'expert').astype(jnp.float32)  56.4 us
    unnamed x2, blocking collectives  54.6 us
    psum x1, waiting for transfers between devices, local(): lax.psum(head_term.astype(jnp.bfloat16), 'expert').astype(jnp.float32)  39 us
    all_gather x1, waiting for transfers between devices, local(): lax.all_gather(up_local, 'dp', axis=0, tiled=True)  37.5 us
    all_gather x1, blocking collectives, local(): all_pooled = lax.all_gather(pooled, 'dp', axis=0, tiled=True)  31.4 us
  transfers between devices with their start and end apart: 7, of which 7 were waited for; matrix products, arithmetic and copies ran while one was open for 6% of the time, Pallas kernels for 0%

commit v1 on v0

--- a/solution.py
+++ b/solution.py
@@ -5,6 +5,19 @@
 
 LISTS = 8
 RANKS = 32
+
+
+def gather_around(x, axis, dim):
+    ways = lax.axis_size(axis)
+    up = [(d, (d + 1) % ways) for d in range(ways)]
+    down = [(d, (d - 1) % ways) for d in range(ways)]
+    earlier, later = ([x], [x])
+    for _ in range(ways // 2):
+        earlier.append(lax.ppermute(earlier[-1], axis, up))
+    for _ in range((ways - 1) // 2):
+        later.append(lax.ppermute(later[-1], axis, down))
+    line = jnp.concatenate([*earlier[::-1], *later[1:]], axis=dim)
+    return jnp.roll(line, (lax.axis_index(axis) - ways // 2) * x.shape[dim], axis=dim)
 
 
 def silu_slope(pre_act):
@@ -93,7 +106,7 @@
         preferred_element_type=jnp.float32,
     )
     pooled = (pooled_sum / token_counts[:, None]).astype(jnp.bfloat16)
-    all_pooled = lax.all_gather(pooled, "dp", axis=0, tiled=True)
+    all_pooled = gather_around(pooled, "dp", 0)
     head_act = jnp.tanh(
         lax.dot_general(
             all_pooled, head_weight, (((1,), (1,)), ((), ())), preferred_element_type=jnp.float32

time: 617 us -> 651 us (1.055)
  starting transfers between devices: 15.7 us -> 68.5 us
  blocking collectives: 201 us -> 173 us
  waiting for transfers between devices: 321 us -> 328 us
    ppermute x0 -> x15, starting transfers between devices: none -> 52.8 us  [the longest x7 35.7 us: gather_around(): later.append(lax.ppermute(later[-1], axis, down))]
    all_gather x1 -> x0, blocking collectives: 31.4 us -> none  [local(): all_pooled = lax.all_gather(pooled, 'dp', axis=0, tiled=True)]
  transfers between devices with their start and end apart: 7 -> 22, of which waited for: 7 -> 9; matrix products, arithmetic and copies ran while one was open for 6% -> 5% of each run, Pallas kernels for 0% -> 0%
where the time goes in v1:
time: 651 us; the launch traced here: 649 us
  waiting for transfers between devices  328 us (50%)
  blocking collectives  173 us (27%)
  starting transfers between devices  68.5 us (11%)
  local copies, waits for them, and re-layouts  27.1 us (4%)
  matrix products  23 us (4%)
  between operations  15.9 us (2%)
  other arithmetic  13.3 us (2%)
    unnamed x6, waiting for transfers between devices  78.3 us
    all_gather x1, waiting for transfers between devices, local(): lax.all_gather(down_local, 'dp', axis=0, tiled=True)  68.4 us
    reduce_scatter x1, waiting for transfers between devices, local(): lax.psum_scatter(jnp.dot(hid_grad, head_weight, preferred_element_type=jn...  65.2 us
    unnamed x2, blocking collectives  59.5 us
    psum x1, blocking collectives, local(): lax.psum(out_term.astype(jnp.bfloat16), 'expert').astype(jnp.float32)  56.4 us
    all_gather x1, waiting for transfers between devices, local(): lax.all_gather(up_local, 'dp', axis=0, tiled=True)  36.7 us
    psum x1, waiting for transfers between devices, local(): lax.psum(head_term.astype(jnp.bfloat16), 'expert').astype(jnp.float32)  36 us
    ppermute x7, starting transfers between devices, gather_around(): later.append(lax.ppermute(later[-1], axis, down))  35.7 us
  transfers between devices with their start and end apart: 22, of which 9 were waited for; matrix products, arithmetic and copies ran while one was open for 5% of the time, Pallas kernels for 0%

profile of v1, /device:TPU:2, one launch (start us, length us, event | category | flops | bytes accessed | tf_op | source)
XLA Modules:
  0.0 649.3 jit_solution(18064722682112697466)
XLA Ops:
  7.2 0.7 all-gather.5.cloned.1.call-update
  8.0 0.7 all-gather.7.cloned.1.call-update
  8.7 0.7 broadcast_multiply_fusion
  9.4 0.8 copy.38
  10.6 1.2 reduce-window.6
  12.2 7.4 %scatter_custom_fusion = bf16[768,1024]{1,0:T(8,128)(2,1)S(1)} fusion(s32[512]{0:T(512)S(1)} %bitcast.66, bf16[128,1024]{1,0:T(8,128)(2,1)} %param.13, s32[1024]{0:T(1024)S(1)} %pad_clamp_fusion.1, bf16[]{:T(256)} %constant.65.clone.1), kind=kCustom, calls=%fused_computation.24 | custom fusion | bytes 1573376 | tf_op jit(solution)/shard_map/scatter | solution.py:58
  19.6 30.3 %all_to_all.15 = bf16[32,24,1024]{2,1,0:T(8,128)(2,1)} all-to-all(bf16[32,24,1024]{2,1,0:T(8,128)(2,1)S(1)} %bitcast.58), channel_id=1, replica_groups=mesh['dp'=16,'expert'=32] {'expert'}, dimensions={0} | all-to-all | bytes 3145728 | tf_op jit(solution)/shard_map/all_to_all | solution.py:60
  49.9 36.7 %all-gather.5.cloned.1.call-done = bf16[1,1024,704]{2,1,0:T(8,128)(2,1)} async-done(((bf16[1,64,704]{2,1,0:T(8,128)(2,1)}), bf16[1,1024,704]{2,1,0:T(8,128)(2,1)}) %all-gather.5.cloned.1.call-update) | async-done | bytes 1441808 | tf_op jit(solution)/shard_map/all_gather | solution.py:74
  86.5 3.2 fusion.2
  89.8 68.4 %all-gather.7.cloned.1.call-done = bf16[1,1024,704]{2,1,0:T(8,128)(2,1)} async-done(((bf16[1,64,704]{2,1,0:T(8,128)(2,1)}), bf16[1,1024,704]{2,1,0:T(8,128)(2,1)}) %all-gather.7.cloned.1.call-update) | async-done | bytes 1441808 | tf_op jit(solution)/shard_map/all_gather | solution.py:80
  158.2 4.1 convolution_convert_fusion
  162.3 7.5 %all-to-all-start.1 = ((bf16[32,24,1024]{2,1,0:T(8,128)(2,1)}), bf16[32,24,1024]{2,1,0:T(8,128)(2,1)S(1)}, u32[]{:S(2)}, u32[]{:S(2)}) async-start(bf16[32,24,1024]{2,1,0:T(8,128)(2,1)} %bitcast.63), calls=%async_computation.1 | async-start | bytes 3145728 | tf_op jit(solution)/shard_map/all_to_all | solution.py:84
  170.3 19.6 %all-to-all-done.1 = bf16[32,24,1024]{2,1,0:T(8,128)(2,1)S(1)} async-done(((bf16[32,24,1024]{2,1,0:T(8,128)(2,1)}), bf16[32,24,1024]{2,1,0:T(8,128)(2,1)S(1)}, u32[]{:S(2)}, u32[]{:S(2)}) %all-to-all-start.1) | async-done | bytes 1572896 | tf_op jit(solution)/shard_map/all_to_all | solution.py:84
  189.9 2.8 gather_fusion
  192.7 1.7 reshape.174
  194.5 1.3 multiply_reduce_fusion
  196.0 0.4 fusion.4
  196.4 3.4 collective-permute-start
  199.9 3.7 collective-permute-done
  203.6 2.1 collective-permute-start.1
  205.7 5.0 collective-permute-start.8
  210.7 1.9 collective-permute-start.2
  212.6 5.1 collective-permute-start.9
  217.7 1.9 collective-permute-start.3
  219.7 5.1 collective-permute-start.10
  224.8 1.9 collective-permute-start.4
  226.8 5.1 collective-permute-start.11
  231.9 1.9 collective-permute-start.5
  233.9 5.1 collective-permute-start.12
  239.0 1.9 collective-permute-start.6
  241.0 5.1 collective-permute-start.13
  246.1 1.9 collective-permute-start.7
  248.3 0.6 fusion.33
  250.2 5.1 collective-permute-start.14
  255.5 1.4 collective-permute-done.14
  257.1 1.0 copy-done.4
  258.1 0.3 multiply_reduce_fusion.4
  258.4 30.5 %all-reduce.1 = f32[256]{0:T(256)S(1)} all-reduce(f32[256]{0:T(256)S(1)} %get-tuple-element.42), channel_id=4, replica_groups=mesh['dp'=16,'expert'=32] {'dp'}, use_global_device_ids=true, to_apply=%region_12.13.clone | all-reduce | flops 256 | bytes 2048
  289.2 27.0 %all-reduce.3 = (f32[8]{0:T(128)S(1)}, f32[8]{0:T(128)S(1)}) all-reduce(f32[8]{0:T(128)S(1)} %get-tuple-element.28, f32[8]{0:T(128)S(1)} %get-tuple-element.27), channel_id=1, replica_groups=mesh['dp'=16,'expert'=32] {'dp'}, use_global_device_ids=true, to_apply=%region_9.10 | all-reduce | flops 16 | bytes 128 | tf_op jit(solution)/shard_map/psum | solution.py:127
  316.5 29.0 %all-reduce.2 = (f32[256]{0:T(256)S(1)}, f32[8]{0:T(128)S(1)}) all-reduce(f32[256]{0:T(256)S(1)} %subtract_dynamic-update-slice_fusion, f32[8]{0:T(128)S(1)} %get-tuple-element.25), channel_id=1, replica_groups=mesh['dp'=16,'expert'=32] {'dp'}, use_global_device_ids=true, to_apply=%add | all-reduce | flops 264 | bytes 2112
  345.5 1.2 convolution_convert_fusion.3
  346.8 65.2 %reduce-scatter.5.cloned.1.call-done = bf16[16,1024]{1,0:T(8,128)(2,1)} async-done(((bf16[256,1024]{1,0:T(8,128)(2,1)}), bf16[16,1024]{1,0:T(8,128)(2,1)}) %reduce-scatter.5.cloned.1.call-update) | async-done | bytes 32784 | tf_op jit(solution)/shard_map/reduce_scatter | solution.py:151
  412.0 1.3 multiply_reduce_fusion.1
  413.5 1.9 mul.211
  415.5 2.0 mul.212
  417.5 3.9 scatter_custom_fusion.1
  421.3 7.6 %all-to-all-start.2 = ((bf16[32,24,1024]{2,1,0:T(8,128)(2,1)}), bf16[32,24,1024]{2,1,0:T(8,128)(2,1)S(1)}, u32[]{:S(2)}, u32[]{:S(2)}) async-start(bf16[32,24,1024]{2,1,0:T(8,128)(2,1)} %bitcast.57), calls=%async_computation.3 | async-start | bytes 3145728 | tf_op jit(solution)/shard_map/all_to_all | solution.py:172
  429.0 0.9 convolution_convert_fusion.4
  430.2 18.9 %all-to-all-done.2 = bf16[32,24,1024]{2,1,0:T(8,128)(2,1)S(1)} async-done(((bf16[32,24,1024]{2,1,0:T(8,128)(2,1)}), bf16[32,24,1024]{2,1,0:T(8,128)(2,1)S(1)}, u32[]{:S(2)}, u32[]{:S(2)}) %all-to-all-start.2) | async-done | bytes 1572896 | tf_op jit(solution)/shard_map/all_to_all | solution.py:172
  449.0 1.2 copy-done.3
  450.3 4.6 convolution_convert_fusion.1
  454.9 7.0 %convolution_convert_fusion.2 = bf16[1024,704]{0,1:T(8,128)(2,1)} fusion(bf16[768,1024]{1,0:T(8,128)(2,1)S(1)} %bitcast.60, f32[768,704]{0,1:T(8,128)} %copy-done.17, bf16[768,1024]{1,0:T(8,128)(2,1)} %bitcast.62, bf16[1,1024,704]{2,1,0:T(8,128)(2,1)} %all-gather.7.cloned.1.call-done), kind=kOutput, calls=%fused_computation.12 | convolution fusion | flops 2220179456 | bytes 8192000 | tf_op jit(solution)/shard_map/dot_general | solution.py:186
  461.9 2.1 pad_maximum_fusion
  464.0 2.9 copy.45
  466.9 0.8 copy-done.7
  467.8 56.4 %psum.38 = bf16[64]{0:T(256)(128)(2,1)S(1)} all-reduce(bf16[64]{0:T(256)(128)(2,1)S(1)} %multiply_reduce_fusion.3), channel_id=1, replica_groups=mesh['dp'=16,'expert'=32] {'expert'}, use_global_device_ids=true, to_apply=%region_22.23 | all-reduce | flops 64 | bytes 256 | tf_op jit(solution)/shard_map/psum | solution.py:149
  524.2 0.5 convert_element_type.88
  524.7 0.6 subtract_reduce_fusion
  525.3 36.0 %all-reduce.6.cloned.1.call-done = bf16[64,1024]{1,0:T(8,128)(2,1)} async-done(((bf16[64,1024]{1,0:T(8,128)(2,1)}), bf16[64,1024]{1,0:T(8,128)(2,1)}) %all-reduce.6.cloned.1.call-update) | async-done | bytes 131088 | tf_op jit(solution)/shard_map/psum | solution.py:148
  561.4 1.6 convert_element_type.86
  563.0 76.8 %reduce-scatter.7.cloned.1.call-done = bf16[64,1408]{1,0:T(8,128)(2,1)} async-done(((bf16[1024,1408]{1,0:T(8,128)(2,1)}), bf16[64,1408]{1,0:T(8,128)(2,1)}) %reduce-scatter.7.cloned.1.call-update) | async-done | bytes 180240
  639.8 1.1 fusion.32
  641.0 0.8 copy.44
  642.0 0.8 copy.43
  (116 shorter events, 3.5 us)
Async XLA Ops:
  7.2 250.9 %copy-start = (bf16[64,1024]{1,0:T(8,128)(2,1)S(1)}, bf16[64,1024]{1,0:T(8,128)(2,1)}, u32[]{:S(2)}) copy-start(bf16[64,1024]{1,0:T(8,128)(2,1)} %param.18) | copy-start | bytes 393220
  7.2 79.4 %all-gather.5.cloned.1.call-start = ((), (), s32[]{:S(2)}) async-start(), calls=%async_computation.7 | async-start | bytes 1671168 | tf_op jit(solution)/shard_map/all_gather | solution.py:74
  7.9 150.2 %all-gather.7.cloned.1.call-start = ((), (), s32[]{:S(2)}) async-start(), calls=%async_computation.8 | async-start | bytes 1671168 | tf_op jit(solution)/shard_map/all_gather | solution.py:80
  89.8 72.5 %copy-start.17 = (f32[768,704]{0,1:T(8,128)}, f32[768,704]{0,1:T(8,128)S(1)}, u32[]{:S(2)}) copy-start(f32[768,704]{0,1:T(8,128)S(1)} %fusion.2) | copy-start | bytes 6488068
  162.2 7.8 %copy-start.9 = (f32[128,4]{0,1:T(4,128)S(1)}, f32[128,4]{0,1:T(4,128)}, u32[]{:S(2)}) copy-start(f32[128,4]{0,1:T(4,128)} %param.15) | copy-start | bytes 6148
  162.3 7.9 %copy-start.11 = (s32[1,128]{1,0:T(1,128)S(1)}, s32[1,128]{1,0:T(1,128)}, u32[]{:S(2)}) copy-start(s32[1,128]{1,0:T(1,128)} %param.20) | copy-start | bytes 1540
  162.3 27.7 %all-to-all-start.1 = ((bf16[32,24,1024]{2,1,0:T(8,128)(2,1)}), bf16[32,24,1024]{2,1,0:T(8,128)(2,1)S(1)}, u32[]{:S(2)}, u32[]{:S(2)}) async-start(bf16[32,24,1024]{2,1,0:T(8,128)(2,1)} %bitcast.63), calls=%async_computation.1 | async-start | bytes 3145728 | tf_op jit(solution)/shard_map/all_to_all | solution.py:84
  169.8 242.2 %reduce-scatter.5.cloned.1.call-start = ((), (), s32[]{:S(2)}) async-start(), calls=%async_computation.5 | async-start | bytes 557056 | tf_op jit(solution)/shard_map/reduce_scatter | solution.py:151
  194.4 1.4 copy-start.1
  194.4 53.6 %copy-start.13 = (f32[32]{0:T(128)S(1)}, f32[32]{0:T(128)}, u32[]{:S(2)}) copy-start(f32[32]{0:T(128)} %param.25) | copy-start | bytes 388
  194.5 53.6 %copy-start.14 = (s32[1,16]{1,0:T(1,128)S(1)}, s32[1,16]{1,0:T(1,128)}, u32[]{:S(2)}) copy-start(s32[1,16]{1,0:T(1,128)} %param.23) | copy-start | bytes 196
  194.5 53.6 %copy-start.15 = (f32[32]{0:T(128)S(1)}, f32[32]{0:T(128)}, u32[]{:S(2)}) copy-start(f32[32]{0:T(128)} %param.24) | copy-start | bytes 388
  194.5 53.8 %copy-start.12 = (u32[512]{0:T(512)S(1)}, u32[512]{0:T(512)}, u32[]{:S(2)}) copy-start(u32[512]{0:T(512)} %constant.95) | copy-start | bytes 6148
  196.0 62.1 %copy-start.8 = (f32[64]{0:T(128)S(1)}, f32[64]{0:T(128)}, u32[]{:S(2)}) copy-start(f32[64]{0:T(128)} %param.19) | copy-start | bytes 772
  196.4 92.5 %copy-start.16 = (s32[1,16]{1,0:T(1,128)S(1)}, s32[1,16]{1,0:T(1,128)}, u32[]{:S(2)}) copy-start(s32[1,16]{1,0:T(1,128)} %param.22) | copy-start | bytes 196
  196.4 92.6 %copy-start.10 = (s32[1,16]{1,0:T(1,128)S(1)}, s32[1,16]{1,0:T(1,128)}, u32[]{:S(2)}) copy-start(s32[1,16]{1,0:T(1,128)} %param.21) | copy-start | bytes 196
  196.4 7.2 %collective-permute-start = (bf16[16,1024]{1,0:T(8,128)(2,1)S(1)}, bf16[16,1024]{1,0:T(8,128)(2,1)S(1)}, u32[]{:S(2)}, u32[]{:S(2)}) collective-permute-start(bf16[16,1024]{1,0:T(8,128)(2,1)S(1)} %fusion.4), channel_id=1, source_target_pairs={{0,32},{32,64},{64,96},{96,128},{128,160},{160,192},{192,224},{224... | collective-permute-start | bytes 98312 | tf_op jit(solution)/shard_map/ppermute | solution.py:16
  203.6 7.1 %collective-permute-start.1 = (bf16[16,1024]{1,0:T(8,128)(2,1)S(1)}, bf16[16,1024]{1,0:T(8,128)(2,1)S(1)}, u32[]{:S(2)}, u32[]{:S(2)}) collective-permute-start(bf16[16,1024]{1,0:T(8,128)(2,1)S(1)} %collective-permute-done), channel_id=1, source_target_pairs={{0,32},{32,64},{64,96},{96,128},{128,160},{160,192},{192,224},{224... | collective-permute-start | bytes 98312 | tf_op jit(solution)/shard_map/ppermute | solution.py:16
  205.7 6.9 %collective-permute-start.8 = (bf16[16,1024]{1,0:T(8,128)(2,1)S(1)}, bf16[16,1024]{1,0:T(8,128)(2,1)S(1)}, u32[]{:S(2)}, u32[]{:S(2)}) collective-permute-start(bf16[16,1024]{1,0:T(8,128)(2,1)S(1)} %fusion.4), channel_id=1, source_target_pairs={{0,480},{32,0},{64,32},{96,64},{128,96},{160,128},{192,160},{224,1... | collective-permute-start | bytes 98312 | tf_op jit(solution)/shard_map/ppermute | solution.py:18
  210.7 7.1 %collective-permute-start.2 = (bf16[16,1024]{1,0:T(8,128)(2,1)S(1)}, bf16[16,1024]{1,0:T(8,128)(2,1)S(1)}, u32[]{:S(2)}, u32[]{:S(2)}) collective-permute-start(bf16[16,1024]{1,0:T(8,128)(2,1)S(1)} %collective-permute-done.1), channel_id=1, source_target_pairs={{0,32},{32,64},{64,96},{96,128},{128,160},{160,192},{192,224},{224... | collective-permute-start | bytes 98312 | tf_op jit(solution)/shard_map/ppermute | solution.py:16
  212.6 7.1 %collective-permute-start.9 = (bf16[16,1024]{1,0:T(8,128)(2,1)S(1)}, bf16[16,1024]{1,0:T(8,128)(2,1)S(1)}, u32[]{:S(2)}, u32[]{:S(2)}) collective-permute-start(bf16[16,1024]{1,0:T(8,128)(2,1)S(1)} %collective-permute-done.8), channel_id=1, source_target_pairs={{0,480},{32,0},{64,32},{96,64},{128,96},{160,128},{192,160},{224,1... | collective-permute-start | bytes 98312 | tf_op jit(solution)/shard_map/ppermute | solution.py:18
  217.7 7.1 %collective-permute-start.3 = (bf16[16,1024]{1,0:T(8,128)(2,1)S(1)}, bf16[16,1024]{1,0:T(8,128)(2,1)S(1)}, u32[]{:S(2)}, u32[]{:S(2)}) collective-permute-start(bf16[16,1024]{1,0:T(8,128)(2,1)S(1)} %collective-permute-done.2), channel_id=1, source_target_pairs={{0,32},{32,64},{64,96},{96,128},{128,160},{160,192},{192,224},{224... | collective-permute-start | bytes 98312 | tf_op jit(solution)/shard_map/ppermute | solution.py:16
  219.7 7.1 %collective-permute-start.10 = (bf16[16,1024]{1,0:T(8,128)(2,1)S(1)}, bf16[16,1024]{1,0:T(8,128)(2,1)S(1)}, u32[]{:S(2)}, u32[]{:S(2)}) collective-permute-start(bf16[16,1024]{1,0:T(8,128)(2,1)S(1)} %collective-permute-done.9), channel_id=1, source_target_pairs={{0,480},{32,0},{64,32},{96,64},{128,96},{160,128},{192,160},{224,1... | collective-permute-start | bytes 98312 | tf_op jit(solution)/shard_map/ppermute | solution.py:18
  224.8 7.1 %collective-permute-start.4 = (bf16[16,1024]{1,0:T(8,128)(2,1)S(1)}, bf16[16,1024]{1,0:T(8,128)(2,1)S(1)}, u32[]{:S(2)}, u32[]{:S(2)}) collective-permute-start(bf16[16,1024]{1,0:T(8,128)(2,1)S(1)} %collective-permute-done.3), channel_id=1, source_target_pairs={{0,32},{32,64},{64,96},{96,128},{128,160},{160,192},{192,224},{224... | collective-permute-start | bytes 98312 | tf_op jit(solution)/shard_map/ppermute | solution.py:16
  226.8 7.1 %collective-permute-start.11 = (bf16[16,1024]{1,0:T(8,128)(2,1)S(1)}, bf16[16,1024]{1,0:T(8,128)(2,1)S(1)}, u32[]{:S(2)}, u32[]{:S(2)}) collective-permute-start(bf16[16,1024]{1,0:T(8,128)(2,1)S(1)} %collective-permute-done.10), channel_id=1, source_target_pairs={{0,480},{32,0},{64,32},{96,64},{128,96},{160,128},{192,160},{224,1... | collective-permute-start | bytes 98312 | tf_op jit(solution)/shard_map/ppermute | solution.py:18
  231.9 7.1 %collective-permute-start.5 = (bf16[16,1024]{1,0:T(8,128)(2,1)S(1)}, bf16[16,1024]{1,0:T(8,128)(2,1)S(1)}, u32[]{:S(2)}, u32[]{:S(2)}) collective-permute-start(bf16[16,1024]{1,0:T(8,128)(2,1)S(1)} %collective-permute-done.4), channel_id=1, source_target_pairs={{0,32},{32,64},{64,96},{96,128},{128,160},{160,192},{192,224},{224... | collective-permute-start | bytes 98312 | tf_op jit(solution)/shard_map/ppermute | solution.py:16
  233.9 7.1 %collective-permute-start.12 = (bf16[16,1024]{1,0:T(8,128)(2,1)S(1)}, bf16[16,1024]{1,0:T(8,128)(2,1)S(1)}, u32[]{:S(2)}, u32[]{:S(2)}) collective-permute-start(bf16[16,1024]{1,0:T(8,128)(2,1)S(1)} %collective-permute-done.11), channel_id=1, source_target_pairs={{0,480},{32,0},{64,32},{96,64},{128,96},{160,128},{192,160},{224,1... | collective-permute-start | bytes 98312 | tf_op jit(solution)/shard_map/ppermute | solution.py:18
  239.0 7.1 %collective-permute-start.6 = (bf16[16,1024]{1,0:T(8,128)(2,1)S(1)}, bf16[16,1024]{1,0:T(8,128)(2,1)S(1)}, u32[]{:S(2)}, u32[]{:S(2)}) collective-permute-start(bf16[16,1024]{1,0:T(8,128)(2,1)S(1)} %collective-permute-done.5), channel_id=1, source_target_pairs={{0,32},{32,64},{64,96},{96,128},{128,160},{160,192},{192,224},{224... | collective-permute-start | bytes 98312 | tf_op jit(solution)/shard_map/ppermute | solution.py:16
  241.0 9.2 %collective-permute-start.13 = (bf16[16,1024]{1,0:T(8,128)(2,1)S(1)}, bf16[16,1024]{1,0:T(8,128)(2,1)S(1)}, u32[]{:S(2)}, u32[]{:S(2)}) collective-permute-start(bf16[16,1024]{1,0:T(8,128)(2,1)S(1)} %collective-permute-done.12), channel_id=1, source_target_pairs={{0,480},{32,0},{64,32},{96,64},{128,96},{160,128},{192,160},{224,1... | collective-permute-start | bytes 98312 | tf_op jit(solution)/shard_map/ppermute | solution.py:18
  246.1 9.2 %collective-permute-start.7 = (bf16[16,1024]{1,0:T(8,128)(2,1)S(1)}, bf16[16,1024]{1,0:T(8,128)(2,1)S(1)}, u32[]{:S(2)}, u32[]{:S(2)}) collective-permute-start(bf16[16,1024]{1,0:T(8,128)(2,1)S(1)} %collective-permute-done.6), channel_id=1, source_target_pairs={{0,32},{32,64},{64,96},{96,128},{128,160},{160,192},{192,224},{224... | collective-permute-start | bytes 98312 | tf_op jit(solution)/shard_map/ppermute | solution.py:16
  250.2 6.7 %collective-permute-start.14 = (bf16[16,1024]{1,0:T(8,128)(2,1)S(1)}, bf16[16,1024]{1,0:T(8,128)(2,1)S(1)}, u32[]{:S(2)}, u32[]{:S(2)}) collective-permute-start(bf16[16,1024]{1,0:T(8,128)(2,1)S(1)} %collective-permute-done.13), channel_id=1, source_target_pairs={{0,480},{32,0},{64,32},{96,64},{128,96},{160,128},{192,160},{224,1... | collective-permute-start | bytes 98312 | tf_op jit(solution)/shard_map/ppermute | solution.py:18
  257.1 1.0 copy-start.4
  258.4 170.6 %copy-start.6 = (f32[256,64]{0,1:T(8,128)}, f32[256,64]{0,1:T(8,128)S(1)}, u32[]{:S(2)}) copy-start(f32[256,64]{0,1:T(8,128)S(1)} %get-tuple-element.43) | copy-start | bytes 196612
  421.3 7.6 %copy-start.5 = (bf16[512,1024]{1,0:T(8,128)(2,1)S(1)}, bf16[512,1024]{1,0:T(8,128)(2,1)}, u32[]{:S(2)}) copy-start(bf16[512,1024]{1,0:T(8,128)(2,1)} %copy-done.4) | copy-start | bytes 3145732
  421.3 27.7 %all-to-all-start.2 = ((bf16[32,24,1024]{2,1,0:T(8,128)(2,1)}), bf16[32,24,1024]{2,1,0:T(8,128)(2,1)S(1)}, u32[]{:S(2)}, u32[]{:S(2)}) async-start(bf16[32,24,1024]{2,1,0:T(8,128)(2,1)} %bitcast.57), calls=%async_computation.3 | async-start | bytes 3145728 | tf_op jit(solution)/shard_map/all_to_all | solution.py:172
  428.9 132.4 %all-reduce.6.cloned.1.call-start = ((), (), s32[]{:S(2)}) async-start(), calls=%async_computation.6 | async-start | bytes 262144 | tf_op jit(solution)/shard_map/psum | solution.py:148
  429.9 209.9 %reduce-scatter.7.cloned.1.call-start = ((), (), s32[]{:S(2)}) async-start(), calls=%async_computation.9 | async-start | bytes 3063808
  449.0 1.2 copy-start.3
  450.3 4.6 copy-start.2
  466.9 0.8 copy-start.7
Sparse Core Ops, SparseCore 0:
  10.1 76.4 all-gather.4
  88.6 69.4 all-gather.6
  346.8 65.1 reduce-scatter.4
  433.6 127.7 all-reduce.5
  564.0 75.7 reduce-scatter.6
